TPU v7x, 512 devices: a whole 4x8x8 slice. The times are simulated.
512 devices in a mesh: section: 16 (over z_lo, x), feat: 32 (over y, z_hi, core).
Axes of the slice: x: 4, y: 8, z: 8 (z_hi: 2, z_lo: 4; z = z_hi * 4 + z_lo), core: 2. Of those that a mesh axis runs over, the one named last changes fastest.
Arguments:
- decoders: bfloat16 [16, 4096, 4608], P('section', 'feat'), may hold values from -0.09375 to 0.09375
- encoders: bfloat16 [16, 4096, 4608], P('section', 'feat'), may hold values from -6 to 6
- out_proj: bfloat16 [16, 4096, 4608], P('section', 'feat'), may hold values from -0.09375 to 0.09375
- value_proj: bfloat16 [16, 4608, 4096], P('section', None, 'feat'), may hold values from -0.09375 to 0.09375
- attention: float32 [16, 32, 16, 16], P('section', 'feat'), may hold values from 0 to 1, as said below
- norm_scale: float32 [16, 16], P('section'), may hold values from 0.05 to 0.5
- act_ids: int32 [16, 4096], P('section'), may hold values from 0 to 4095, as said below
- act_values: float32 [16, 4096], P('section', 'feat'), may hold values from 0.1 to 10
- target_ids: int32 [64], P('section'), may hold values from 0 to 4095
- target_pos: int32 [64], P('section'), may hold values from 0 to 15
Outputs:
- edges: float32 [16, 64, 4096], P('section', None, 'feat')
Inputs may be any that keep to these rules, and one draw needn't show every extreme that they name: Every row attention[l, h, p, :] is nonnegative, zero at keys after p, and sums to one. `act_ids`: A feature id f is held by shard f // 128 of feat. In each aligned block of 128 entries of a layer (the entries of one device), at most 8 ids lie in one shard, and in every block some shard has exactly 8.
All inputs are finite; a program needn't handle non-finite values.
Results may differ from a plain program's by a relative error of at most 0.015.
Values may be sent and summed in bfloat16 or wider, within the bound.
No kernel may reach another device: no remote copies, remote signals or barrier semaphores. Data moves between devices by JAX's collectives and lax.ppermute only.
A program may use at most 64 MiB of HBM per device.

v0:
```python
import jax
import jax.numpy as jnp
from jax import lax
from jax.sharding import PartitionSpec as P

K_ACT = 256


def shifted(shard, axis, by):
    length = lax.axis_size(axis)
    pairs = [(i, i + by) for i in range(length) if 0 <= i + by < length]
    return lax.ppermute(shard, axis, pairs)


def per_device(
    decoders,
    encoders,
    out_proj,
    value_proj,
    attention,
    norm_scale,
    act_ids,
    act_values,
    target_ids,
    target_pos,
):
    feat_count = lax.axis_size("feat")
    section_count = lax.axis_size("section")
    feat_index = lax.axis_index("feat")
    section_index = lax.axis_index("section")
    dec_table = decoders[0]
    enc_table = encoders[0]
    out_weight = out_proj[0]
    value_weight = value_proj[0]
    mixing = attention[0, 0]
    scales = norm_scale[0]
    act_weights = act_values[0]
    feat_rows = dec_table.shape[0]
    model_width = dec_table.shape[1]
    head_width = out_weight.shape[0]
    seq_len = mixing.shape[0]
    batch_size = target_ids.shape[0]
    entries_dev = act_weights.shape[0]
    slot_count = 2 * entries_dev // feat_count
    rows_all = batch_size * seq_len
    rows_dev = rows_all // feat_count
    ids_blocks = act_ids[0].reshape(feat_count, entries_dev)
    owner_ids = ids_blocks // feat_rows
    local_ids = ids_blocks % feat_rows
    owned_mask = (owner_ids == feat_index).astype(jnp.int32)
    slot_rank = jnp.cumsum(owned_mask, axis=1) - 1
    slot_iota = jnp.arange(slot_count, dtype=jnp.int32)
    selected = owned_mask[:, None, :] * (slot_rank[:, None, :] == slot_iota[None, :, None]).astype(
        jnp.int32
    )
    source_row = jnp.sum(selected * local_ids[:, None, :], axis=2)
    is_filled = jnp.sum(selected, axis=2)
    entry_iota = jnp.arange(entries_dev, dtype=jnp.int32)
    outgoing = jnp.take(dec_table, source_row.reshape(-1), axis=0).reshape(
        feat_count, slot_count, model_width
    )
    outgoing = jnp.where(is_filled[:, :, None] > 0, outgoing, jnp.zeros_like(outgoing))
    own_owner = lax.dynamic_index_in_dim(owner_ids, feat_index, 0, keepdims=False)
    earlier = (entry_iota[None, :] < entry_iota[:, None]).astype(jnp.int32)
    same_owner = (own_owner[:, None] == own_owner[None, :]).astype(jnp.int32)
    own_rank = jnp.sum(earlier * same_owner, axis=1)
    flat_index = own_owner * slot_count + own_rank
    positions = jnp.arange(seq_len, dtype=jnp.int32)
    incoming = lax.all_to_all(outgoing, "feat", split_axis=0, concat_axis=0, tiled=True)
    partners = jnp.take(incoming.reshape(feat_count * slot_count, model_width), flat_index, axis=0)
    own_pos = (feat_index * entries_dev + entry_iota) // K_ACT
    edge_pick = (positions[:, None] == own_pos[None, :]).astype(jnp.float32)
    feat_iota = jnp.arange(feat_rows, dtype=jnp.int32)
    target_pick = ((target_ids - feat_index * feat_rows)[:, None] == feat_iota[None, :]).astype(
        jnp.bfloat16
    )
    enc_part = jnp.dot(target_pick, enc_table, preferred_element_type=jnp.float32)
    enc_full = lax.psum(enc_part.astype(jnp.bfloat16), "feat").astype(jnp.float32)
    row_iota = feat_index * rows_dev + jnp.arange(rows_dev, dtype=jnp.int32)
    row_target = row_iota // seq_len
    row_pos = row_iota % seq_len
    target_onehot = (
        row_target[:, None] == jnp.arange(batch_size, dtype=jnp.int32)[None, :]
    ).astype(jnp.float32)
    row_enc = jnp.dot(target_onehot, enc_full, precision=lax.Precision.HIGHEST)
    row_hit = jnp.sum(
        target_onehot * (row_pos[:, None] == target_pos[None, :]).astype(jnp.float32), axis=1
    )
    start_rows = row_enc * row_hit[:, None]
    scale_rows = jnp.tile(scales, batch_size)

    def produce(shard_rows):
        head_part = lax.dot_general(
            shard_rows, out_weight, (((1,), (1,)), ((), ())), preferred_element_type=jnp.float32
        )
        edge_part = lax.dot_general(
            shard_rows, partners, (((1,), (1,)), ((), ())), preferred_element_type=jnp.float32
        )
        return jnp.concatenate([head_part, edge_part], axis=1)

    def gathered_products(adjoint_rows):
        joined = produce(
            lax.all_gather(adjoint_rows.astype(jnp.bfloat16), "feat", axis=0, tiled=True)
        )
        return (joined[:, :head_width], joined[:, head_width:])

    def record(edges_out, edge_raw, step_num):
        edge_vals = jnp.sum(edge_raw.reshape(batch_size, seq_len, -1) * edge_pick[None], axis=1)
        edge_vals = edge_vals * act_weights[None, :]
        batch_num = section_index + step_num
        in_range = batch_num < section_count
        row_start = jnp.minimum(batch_num, section_count - 1) * batch_size
        current = lax.dynamic_slice_in_dim(edges_out, row_start, batch_size, 0)
        updated = jnp.where(in_range, edge_vals, current)
        return lax.dynamic_update_slice_in_dim(edges_out, updated, row_start, 0)

    def propagate(adjoint_rows, head_grad):
        mixed_rows = jnp.einsum(
            "pq,tph->tqh", mixing, head_grad.reshape(batch_size, seq_len, head_width)
        )
        mixed_rows = mixed_rows.astype(jnp.bfloat16).reshape(rows_all, head_width)
        head_term = lax.dot_general(
            mixed_rows, value_weight, (((1,), (1,)), ((), ())), preferred_element_type=jnp.float32
        )
        head_term = (head_term * scale_rows[:, None]).astype(jnp.bfloat16)
        head_parts = lax.all_to_all(
            head_term.reshape(feat_count, rows_dev, model_width),
            "feat",
            split_axis=0,
            concat_axis=0,
            tiled=True,
        )
        return adjoint_rows + jnp.sum(head_parts.astype(jnp.float32), axis=0)

    def one_hop(step_num, loop_state):
        adjoint_rows, edges_out = loop_state
        head_grad, edge_raw = gathered_products(adjoint_rows)
        edges_out = record(edges_out, edge_raw, step_num)
        adjoint_rows = propagate(adjoint_rows, head_grad)
        adjoint_rows = shifted(adjoint_rows, "section", -1)
        return (adjoint_rows, edges_out)

    blank_edges = jnp.zeros((batch_size * section_count, entries_dev), jnp.float32)
    adjoint_rows, edges_out = lax.fori_loop(
        0, section_count - 1, one_hop, (start_rows, blank_edges)
    )
    unused, edge_raw = gathered_products(adjoint_rows)
    edges_out = record(edges_out, edge_raw, section_count - 1)
    return edges_out[None]


def solution(mesh):
    in_specs = (
        P("section", "feat", None),
        P("section", "feat", None),
        P("section", "feat", None),
        P("section", None, "feat"),
        P("section", "feat", None, None),
        P("section", None),
        P("section", None),
        P("section", "feat"),
        P("section"),
        P("section"),
    )
    out_specs = P("section", None, "feat")
    return jax.shard_map(
        per_device, mesh=mesh, in_specs=in_specs, out_specs=out_specs, check_vma=False
    )
```

profile of v0, /device:TPU:7, one launch (start us, length us, event | category | flops | bytes accessed | tf_op | source)
XLA Modules:
  0.0 1708.6 jit_solution(6113719031879558442)
XLA Ops:
  27.0 205.2 %psum.7 = bf16[4,4608]{1,0:T(4,128)(2,1)} all-reduce(bf16[4,4608]{1,0:T(4,128)(2,1)} %convolution_convert_fusion.1), channel_id=1, replica_groups=mesh['section'=16,'feat'=32] {'feat'}, use_global_device_ids=true, to_apply=%region_0.1 | all-reduce | flops 18432 | bytes 73728 | tf_op jit(solution)/shard_map/psum | solution.py:78
  243.1 1407.9 %while.16 = (s32[]{:T(128)}, f32[2,4608]{1,0:T(2,128)S(1)}, f32[64,128]{1,0:T(8,128)}, bf16[128,4608]{1,0:T(8,128)(2,1)}, bf16[16,16]{0,1:T(8,128)(2,1)S(1)}, /*...) while((s32[]{:T(128)}, f32[2,4608]{1,0:T(2,128)S(1)}, ...), condition=%wide.region_9.10_spmd.clone, body=%wide.region_6.9_spmd.clone.sunk | while | flops 227964416 | bytes 15944625 | solution.py:144
  243.7 56.5 %all-gather.4 = bf16[32,2,4608]{2,1,0:T(2,128)(2,1)S(1)} all-gather(bf16[1,2,4608]{2,1,0:T(2,128)(2,1)S(1)} %convert_bitcast_fusion.3), channel_id=1, replica_groups=mesh['section'=16,'feat'=32] {'feat'}, dimensions={0}, use_global_device_ids=true | all-gather | bytes 608256 | tf_op jit(solution)/shard_map/while/body/eval_jaxpr/all_gather | solution.py:103
  316.3 19.1 %all-to-all-done = bf16[32,2,4608]{2,1,0:T(2,128)(2,1)S(1)} async-done(((bf16[32,2,4608]{2,1,0:T(2,128)(2,1)}), bf16[32,2,4608]{2,1,0:T(2,128)(2,1)S(1)}, u32[]{:S(2)}, u32[]{:S(2)}) %all-to-all-start) | async-done | bytes 589856 | tf_op jit(solution)/shard_map/while/body/eval_jaxpr/all_to_all | solution.py:126
  344.0 53.4 %all-gather.4 = bf16[32,2,4608]{2,1,0:T(2,128)(2,1)S(1)} all-gather(bf16[1,2,4608]{2,1,0:T(2,128)(2,1)S(1)} %convert_bitcast_fusion.3), channel_id=1, replica_groups=mesh['section'=16,'feat'=32] {'feat'}, dimensions={0}, use_global_device_ids=true | all-gather | bytes 608256 | tf_op jit(solution)/shard_map/while/body/eval_jaxpr/all_gather | solution.py:103
  410.3 18.7 %all-to-all-done = bf16[32,2,4608]{2,1,0:T(2,128)(2,1)S(1)} async-done(((bf16[32,2,4608]{2,1,0:T(2,128)(2,1)}), bf16[32,2,4608]{2,1,0:T(2,128)(2,1)S(1)}, u32[]{:S(2)}, u32[]{:S(2)}) %all-to-all-start) | async-done | bytes 589856 | tf_op jit(solution)/shard_map/while/body/eval_jaxpr/all_to_all | solution.py:126
  437.7 54.1 %all-gather.4 = bf16[32,2,4608]{2,1,0:T(2,128)(2,1)S(1)} all-gather(bf16[1,2,4608]{2,1,0:T(2,128)(2,1)S(1)} %convert_bitcast_fusion.3), channel_id=1, replica_groups=mesh['section'=16,'feat'=32] {'feat'}, dimensions={0}, use_global_device_ids=true | all-gather | bytes 608256 | tf_op jit(solution)/shard_map/while/body/eval_jaxpr/all_gather | solution.py:103
  531.1 54.1 %all-gather.4 = bf16[32,2,4608]{2,1,0:T(2,128)(2,1)S(1)} all-gather(bf16[1,2,4608]{2,1,0:T(2,128)(2,1)S(1)} %convert_bitcast_fusion.3), channel_id=1, replica_groups=mesh['section'=16,'feat'=32] {'feat'}, dimensions={0}, use_global_device_ids=true | all-gather | bytes 608256 | tf_op jit(solution)/shard_map/while/body/eval_jaxpr/all_gather | solution.py:103
  597.1 18.7 %all-to-all-done = bf16[32,2,4608]{2,1,0:T(2,128)(2,1)S(1)} async-done(((bf16[32,2,4608]{2,1,0:T(2,128)(2,1)}), bf16[32,2,4608]{2,1,0:T(2,128)(2,1)S(1)}, u32[]{:S(2)}, u32[]{:S(2)}) %all-to-all-start) | async-done | bytes 589856 | tf_op jit(solution)/shard_map/while/body/eval_jaxpr/all_to_all | solution.py:126
  624.5 54.1 %all-gather.4 = bf16[32,2,4608]{2,1,0:T(2,128)(2,1)S(1)} all-gather(bf16[1,2,4608]{2,1,0:T(2,128)(2,1)S(1)} %convert_bitcast_fusion.3), channel_id=1, replica_groups=mesh['section'=16,'feat'=32] {'feat'}, dimensions={0}, use_global_device_ids=true | all-gather | bytes 608256 | tf_op jit(solution)/shard_map/while/body/eval_jaxpr/all_gather | solution.py:103
  690.5 18.7 %all-to-all-done = bf16[32,2,4608]{2,1,0:T(2,128)(2,1)S(1)} async-done(((bf16[32,2,4608]{2,1,0:T(2,128)(2,1)}), bf16[32,2,4608]{2,1,0:T(2,128)(2,1)S(1)}, u32[]{:S(2)}, u32[]{:S(2)}) %all-to-all-start) | async-done | bytes 589856 | tf_op jit(solution)/shard_map/while/body/eval_jaxpr/all_to_all | solution.py:126
  717.8 54.2 %all-gather.4 = bf16[32,2,4608]{2,1,0:T(2,128)(2,1)S(1)} all-gather(bf16[1,2,4608]{2,1,0:T(2,128)(2,1)S(1)} %convert_bitcast_fusion.3), channel_id=1, replica_groups=mesh['section'=16,'feat'=32] {'feat'}, dimensions={0}, use_global_device_ids=true | all-gather | bytes 608256 | tf_op jit(solution)/shard_map/while/body/eval_jaxpr/all_gather | solution.py:103
  783.8 18.7 %all-to-all-done = bf16[32,2,4608]{2,1,0:T(2,128)(2,1)S(1)} async-done(((bf16[32,2,4608]{2,1,0:T(2,128)(2,1)}), bf16[32,2,4608]{2,1,0:T(2,128)(2,1)S(1)}, u32[]{:S(2)}, u32[]{:S(2)}) %all-to-all-start) | async-done | bytes 589856 | tf_op jit(solution)/shard_map/while/body/eval_jaxpr/all_to_all | solution.py:126
  811.2 54.2 %all-gather.4 = bf16[32,2,4608]{2,1,0:T(2,128)(2,1)S(1)} all-gather(bf16[1,2,4608]{2,1,0:T(2,128)(2,1)S(1)} %convert_bitcast_fusion.3), channel_id=1, replica_groups=mesh['section'=16,'feat'=32] {'feat'}, dimensions={0}, use_global_device_ids=true | all-gather | bytes 608256 | tf_op jit(solution)/shard_map/while/body/eval_jaxpr/all_gather | solution.py:103
  877.2 18.7 %all-to-all-done = bf16[32,2,4608]{2,1,0:T(2,128)(2,1)S(1)} async-done(((bf16[32,2,4608]{2,1,0:T(2,128)(2,1)}), bf16[32,2,4608]{2,1,0:T(2,128)(2,1)S(1)}, u32[]{:S(2)}, u32[]{:S(2)}) %all-to-all-start) | async-done | bytes 589856 | tf_op jit(solution)/shard_map/while/body/eval_jaxpr/all_to_all | solution.py:126
  904.6 54.2 %all-gather.4 = bf16[32,2,4608]{2,1,0:T(2,128)(2,1)S(1)} all-gather(bf16[1,2,4608]{2,1,0:T(2,128)(2,1)S(1)} %convert_bitcast_fusion.3), channel_id=1, replica_groups=mesh['section'=16,'feat'=32] {'feat'}, dimensions={0}, use_global_device_ids=true | all-gather | bytes 608256 | tf_op jit(solution)/shard_map/while/body/eval_jaxpr/all_gather | solution.py:103
  970.6 18.7 %all-to-all-done = bf16[32,2,4608]{2,1,0:T(2,128)(2,1)S(1)} async-done(((bf16[32,2,4608]{2,1,0:T(2,128)(2,1)}), bf16[32,2,4608]{2,1,0:T(2,128)(2,1)S(1)}, u32[]{:S(2)}, u32[]{:S(2)}) %all-to-all-start) | async-done | bytes 589856 | tf_op jit(solution)/shard_map/while/body/eval_jaxpr/all_to_all | solution.py:126
  998.0 54.2 %all-gather.4 = bf16[32,2,4608]{2,1,0:T(2,128)(2,1)S(1)} all-gather(bf16[1,2,4608]{2,1,0:T(2,128)(2,1)S(1)} %convert_bitcast_fusion.3), channel_id=1, replica_groups=mesh['section'=16,'feat'=32] {'feat'}, dimensions={0}, use_global_device_ids=true | all-gather | bytes 608256 | tf_op jit(solution)/shard_map/while/body/eval_jaxpr/all_gather | solution.py:103
  1064.0 18.7 %all-to-all-done = bf16[32,2,4608]{2,1,0:T(2,128)(2,1)S(1)} async-done(((bf16[32,2,4608]{2,1,0:T(2,128)(2,1)}), bf16[32,2,4608]{2,1,0:T(2,128)(2,1)S(1)}, u32[]{:S(2)}, u32[]{:S(2)}) %all-to-all-start) | async-done | bytes 589856 | tf_op jit(solution)/shard_map/while/body/eval_jaxpr/all_to_all | solution.py:126
  1091.3 54.2 %all-gather.4 = bf16[32,2,4608]{2,1,0:T(2,128)(2,1)S(1)} all-gather(bf16[1,2,4608]{2,1,0:T(2,128)(2,1)S(1)} %convert_bitcast_fusion.3), channel_id=1, replica_groups=mesh['section'=16,'feat'=32] {'feat'}, dimensions={0}, use_global_device_ids=true | all-gather | bytes 608256 | tf_op jit(solution)/shard_map/while/body/eval_jaxpr/all_gather | solution.py:103
  1157.3 18.7 %all-to-all-done = bf16[32,2,4608]{2,1,0:T(2,128)(2,1)S(1)} async-done(((bf16[32,2,4608]{2,1,0:T(2,128)(2,1)}), bf16[32,2,4608]{2,1,0:T(2,128)(2,1)S(1)}, u32[]{:S(2)}, u32[]{:S(2)}) %all-to-all-start) | async-done | bytes 589856 | tf_op jit(solution)/shard_map/while/body/eval_jaxpr/all_to_all | solution.py:126
  1184.7 54.2 %all-gather.4 = bf16[32,2,4608]{2,1,0:T(2,128)(2,1)S(1)} all-gather(bf16[1,2,4608]{2,1,0:T(2,128)(2,1)S(1)} %convert_bitcast_fusion.3), channel_id=1, replica_groups=mesh['section'=16,'feat'=32] {'feat'}, dimensions={0}, use_global_device_ids=true | all-gather | bytes 608256 | tf_op jit(solution)/shard_map/while/body/eval_jaxpr/all_gather | solution.py:103
  1250.7 18.7 %all-to-all-done = bf16[32,2,4608]{2,1,0:T(2,128)(2,1)S(1)} async-done(((bf16[32,2,4608]{2,1,0:T(2,128)(2,1)}), bf16[32,2,4608]{2,1,0:T(2,128)(2,1)S(1)}, u32[]{:S(2)}, u32[]{:S(2)}) %all-to-all-start) | async-done | bytes 589856 | tf_op jit(solution)/shard_map/while/body/eval_jaxpr/all_to_all | solution.py:126
  1278.1 54.2 %all-gather.4 = bf16[32,2,4608]{2,1,0:T(2,128)(2,1)S(1)} all-gather(bf16[1,2,4608]{2,1,0:T(2,128)(2,1)S(1)} %convert_bitcast_fusion.3), channel_id=1, replica_groups=mesh['section'=16,'feat'=32] {'feat'}, dimensions={0}, use_global_device_ids=true | all-gather | bytes 608256 | tf_op jit(solution)/shard_map/while/body/eval_jaxpr/all_gather | solution.py:103
  1344.1 18.7 %all-to-all-done = bf16[32,2,4608]{2,1,0:T(2,128)(2,1)S(1)} async-done(((bf16[32,2,4608]{2,1,0:T(2,128)(2,1)}), bf16[32,2,4608]{2,1,0:T(2,128)(2,1)S(1)}, u32[]{:S(2)}, u32[]{:S(2)}) %all-to-all-start) | async-done | bytes 589856 | tf_op jit(solution)/shard_map/while/body/eval_jaxpr/all_to_all | solution.py:126
  1371.4 54.2 %all-gather.4 = bf16[32,2,4608]{2,1,0:T(2,128)(2,1)S(1)} all-gather(bf16[1,2,4608]{2,1,0:T(2,128)(2,1)S(1)} %convert_bitcast_fusion.3), channel_id=1, replica_groups=mesh['section'=16,'feat'=32] {'feat'}, dimensions={0}, use_global_device_ids=true | all-gather | bytes 608256 | tf_op jit(solution)/shard_map/while/body/eval_jaxpr/all_gather | solution.py:103
  1437.5 18.7 %all-to-all-done = bf16[32,2,4608]{2,1,0:T(2,128)(2,1)S(1)} async-done(((bf16[32,2,4608]{2,1,0:T(2,128)(2,1)}), bf16[32,2,4608]{2,1,0:T(2,128)(2,1)S(1)}, u32[]{:S(2)}, u32[]{:S(2)}) %all-to-all-start) | async-done | bytes 589856 | tf_op jit(solution)/shard_map/while/body/eval_jaxpr/all_to_all | solution.py:126
  1464.8 54.2 %all-gather.4 = bf16[32,2,4608]{2,1,0:T(2,128)(2,1)S(1)} all-gather(bf16[1,2,4608]{2,1,0:T(2,128)(2,1)S(1)} %convert_bitcast_fusion.3), channel_id=1, replica_groups=mesh['section'=16,'feat'=32] {'feat'}, dimensions={0}, use_global_device_ids=true | all-gather | bytes 608256 | tf_op jit(solution)/shard_map/while/body/eval_jaxpr/all_gather | solution.py:103
  1530.8 18.7 %all-to-all-done = bf16[32,2,4608]{2,1,0:T(2,128)(2,1)S(1)} async-done(((bf16[32,2,4608]{2,1,0:T(2,128)(2,1)}), bf16[32,2,4608]{2,1,0:T(2,128)(2,1)S(1)}, u32[]{:S(2)}, u32[]{:S(2)}) %all-to-all-start) | async-done | bytes 589856 | tf_op jit(solution)/shard_map/while/body/eval_jaxpr/all_to_all | solution.py:126
  1558.2 54.2 %all-gather.4 = bf16[32,2,4608]{2,1,0:T(2,128)(2,1)S(1)} all-gather(bf16[1,2,4608]{2,1,0:T(2,128)(2,1)S(1)} %convert_bitcast_fusion.3), channel_id=1, replica_groups=mesh['section'=16,'feat'=32] {'feat'}, dimensions={0}, use_global_device_ids=true | all-gather | bytes 608256 | tf_op jit(solution)/shard_map/while/body/eval_jaxpr/all_gather | solution.py:103
  1624.2 18.7 %all-to-all-done = bf16[32,2,4608]{2,1,0:T(2,128)(2,1)S(1)} async-done(((bf16[32,2,4608]{2,1,0:T(2,128)(2,1)}), bf16[32,2,4608]{2,1,0:T(2,128)(2,1)S(1)}, u32[]{:S(2)}, u32[]{:S(2)}) %all-to-all-start) | async-done | bytes 589856 | tf_op jit(solution)/shard_map/while/body/eval_jaxpr/all_to_all | solution.py:126
  1651.0 54.2 %all-gather.1 = bf16[32,2,4608]{2,1,0:T(2,128)(2,1)S(1)} all-gather(bf16[1,2,4608]{2,1,0:T(2,128)(2,1)S(1)} %convert_bitcast_fusion.1), channel_id=1, replica_groups=mesh['section'=16,'feat'=32] {'feat'}, dimensions={0}, use_global_device_ids=true | all-gather | bytes 608256 | tf_op jit(solution)/shard_map/all_gather | solution.py:103
  (344 shorter events, 371.9 us)
Async XLA Ops:
  7.6 16.5 copy-start.5
  7.6 231.2 %all-to-all-start.1 = ((bf16[32,8,4608]{2,1,0:T(8,128)(2,1)}), bf16[32,8,4608]{2,1,0:T(8,128)(2,1)S(1)}, u32[]{:S(2)}, u32[]{:S(2)}) async-start(bf16[32,8,4608]{2,1,0:T(8,128)(2,1)} %fusion.7), calls=%async_computation.1 | async-start | bytes 4718592 | tf_op jit(solution)/shard_map/all_to_all | solution.py:69
  304.7 30.6 %all-to-all-start = ((bf16[32,2,4608]{2,1,0:T(2,128)(2,1)}), bf16[32,2,4608]{2,1,0:T(2,128)(2,1)S(1)}, u32[]{:S(2)}, u32[]{:S(2)}) async-start(bf16[32,2,4608]{2,1,0:T(2,128)(2,1)} %reshape.317), calls=%async_computation | async-start | bytes 1179648 | tf_op jit(solution)/shard_map/while/body/eval_jaxpr/all_to_all | solution.py:126
  336.6 6.8 collective-permute-start
  402.0 27.0 %all-to-all-start = ((bf16[32,2,4608]{2,1,0:T(2,128)(2,1)}), bf16[32,2,4608]{2,1,0:T(2,128)(2,1)S(1)}, u32[]{:S(2)}, u32[]{:S(2)}) async-start(bf16[32,2,4608]{2,1,0:T(2,128)(2,1)} %reshape.317), calls=%async_computation | async-start | bytes 1179648 | tf_op jit(solution)/shard_map/while/body/eval_jaxpr/all_to_all | solution.py:126
  430.3 6.8 collective-permute-start
  496.3 26.1 %all-to-all-start = ((bf16[32,2,4608]{2,1,0:T(2,128)(2,1)}), bf16[32,2,4608]{2,1,0:T(2,128)(2,1)S(1)}, u32[]{:S(2)}, u32[]{:S(2)}) async-start(bf16[32,2,4608]{2,1,0:T(2,128)(2,1)} %reshape.317), calls=%async_computation | async-start | bytes 1179648 | tf_op jit(solution)/shard_map/while/body/eval_jaxpr/all_to_all | solution.py:126
  523.7 6.8 collective-permute-start
  589.7 26.1 %all-to-all-start = ((bf16[32,2,4608]{2,1,0:T(2,128)(2,1)}), bf16[32,2,4608]{2,1,0:T(2,128)(2,1)S(1)}, u32[]{:S(2)}, u32[]{:S(2)}) async-start(bf16[32,2,4608]{2,1,0:T(2,128)(2,1)} %reshape.317), calls=%async_computation | async-start | bytes 1179648 | tf_op jit(solution)/shard_map/while/body/eval_jaxpr/all_to_all | solution.py:126
  617.1 6.8 collective-permute-start
  683.1 26.0 %all-to-all-start = ((bf16[32,2,4608]{2,1,0:T(2,128)(2,1)}), bf16[32,2,4608]{2,1,0:T(2,128)(2,1)S(1)}, u32[]{:S(2)}, u32[]{:S(2)}) async-start(bf16[32,2,4608]{2,1,0:T(2,128)(2,1)} %reshape.317), calls=%async_computation | async-start | bytes 1179648 | tf_op jit(solution)/shard_map/while/body/eval_jaxpr/all_to_all | solution.py:126
  710.4 6.8 collective-permute-start
  776.6 25.9 %all-to-all-start = ((bf16[32,2,4608]{2,1,0:T(2,128)(2,1)}), bf16[32,2,4608]{2,1,0:T(2,128)(2,1)S(1)}, u32[]{:S(2)}, u32[]{:S(2)}) async-start(bf16[32,2,4608]{2,1,0:T(2,128)(2,1)} %reshape.317), calls=%async_computation | async-start | bytes 1179648 | tf_op jit(solution)/shard_map/while/body/eval_jaxpr/all_to_all | solution.py:126
  803.8 6.8 collective-permute-start
  870.0 25.9 %all-to-all-start = ((bf16[32,2,4608]{2,1,0:T(2,128)(2,1)}), bf16[32,2,4608]{2,1,0:T(2,128)(2,1)S(1)}, u32[]{:S(2)}, u32[]{:S(2)}) async-start(bf16[32,2,4608]{2,1,0:T(2,128)(2,1)} %reshape.317), calls=%async_computation | async-start | bytes 1179648 | tf_op jit(solution)/shard_map/while/body/eval_jaxpr/all_to_all | solution.py:126
  897.2 6.8 collective-permute-start
  963.3 26.0 %all-to-all-start = ((bf16[32,2,4608]{2,1,0:T(2,128)(2,1)}), bf16[32,2,4608]{2,1,0:T(2,128)(2,1)S(1)}, u32[]{:S(2)}, u32[]{:S(2)}) async-start(bf16[32,2,4608]{2,1,0:T(2,128)(2,1)} %reshape.317), calls=%async_computation | async-start | bytes 1179648 | tf_op jit(solution)/shard_map/while/body/eval_jaxpr/all_to_all | solution.py:126
  990.5 6.8 collective-permute-start
  1056.7 25.9 %all-to-all-start = ((bf16[32,2,4608]{2,1,0:T(2,128)(2,1)}), bf16[32,2,4608]{2,1,0:T(2,128)(2,1)S(1)}, u32[]{:S(2)}, u32[]{:S(2)}) async-start(bf16[32,2,4608]{2,1,0:T(2,128)(2,1)} %reshape.317), calls=%async_computation | async-start | bytes 1179648 | tf_op jit(solution)/shard_map/while/body/eval_jaxpr/all_to_all | solution.py:126
  1083.9 6.8 collective-permute-start
  1150.1 26.0 %all-to-all-start = ((bf16[32,2,4608]{2,1,0:T(2,128)(2,1)}), bf16[32,2,4608]{2,1,0:T(2,128)(2,1)S(1)}, u32[]{:S(2)}, u32[]{:S(2)}) async-start(bf16[32,2,4608]{2,1,0:T(2,128)(2,1)} %reshape.317), calls=%async_computation | async-start | bytes 1179648 | tf_op jit(solution)/shard_map/while/body/eval_jaxpr/all_to_all | solution.py:126
  1177.3 6.8 collective-permute-start
  1243.5 25.9 %all-to-all-start = ((bf16[32,2,4608]{2,1,0:T(2,128)(2,1)}), bf16[32,2,4608]{2,1,0:T(2,128)(2,1)S(1)}, u32[]{:S(2)}, u32[]{:S(2)}) async-start(bf16[32,2,4608]{2,1,0:T(2,128)(2,1)} %reshape.317), calls=%async_computation | async-start | bytes 1179648 | tf_op jit(solution)/shard_map/while/body/eval_jaxpr/all_to_all | solution.py:126
  1270.7 6.8 collective-permute-start
  1336.8 26.0 %all-to-all-start = ((bf16[32,2,4608]{2,1,0:T(2,128)(2,1)}), bf16[32,2,4608]{2,1,0:T(2,128)(2,1)S(1)}, u32[]{:S(2)}, u32[]{:S(2)}) async-start(bf16[32,2,4608]{2,1,0:T(2,128)(2,1)} %reshape.317), calls=%async_computation | async-start | bytes 1179648 | tf_op jit(solution)/shard_map/while/body/eval_jaxpr/all_to_all | solution.py:126
  1364.0 6.8 collective-permute-start
  1430.2 25.9 %all-to-all-start = ((bf16[32,2,4608]{2,1,0:T(2,128)(2,1)}), bf16[32,2,4608]{2,1,0:T(2,128)(2,1)S(1)}, u32[]{:S(2)}, u32[]{:S(2)}) async-start(bf16[32,2,4608]{2,1,0:T(2,128)(2,1)} %reshape.317), calls=%async_computation | async-start | bytes 1179648 | tf_op jit(solution)/shard_map/while/body/eval_jaxpr/all_to_all | solution.py:126
  1457.4 6.8 collective-permute-start
  1523.5 26.0 %all-to-all-start = ((bf16[32,2,4608]{2,1,0:T(2,128)(2,1)}), bf16[32,2,4608]{2,1,0:T(2,128)(2,1)S(1)}, u32[]{:S(2)}, u32[]{:S(2)}) async-start(bf16[32,2,4608]{2,1,0:T(2,128)(2,1)} %reshape.317), calls=%async_computation | async-start | bytes 1179648 | tf_op jit(solution)/shard_map/while/body/eval_jaxpr/all_to_all | solution.py:126
  1550.8 6.8 collective-permute-start
  1616.9 25.9 %all-to-all-start = ((bf16[32,2,4608]{2,1,0:T(2,128)(2,1)}), bf16[32,2,4608]{2,1,0:T(2,128)(2,1)S(1)}, u32[]{:S(2)}, u32[]{:S(2)}) async-start(bf16[32,2,4608]{2,1,0:T(2,128)(2,1)} %reshape.317), calls=%async_computation | async-start | bytes 1179648 | tf_op jit(solution)/shard_map/while/body/eval_jaxpr/all_to_all | solution.py:126
  1644.1 6.8 collective-permute-start
  (33 other events, 46.8 us)
where the time goes:
time: 1710 us
  blocking collectives  1070 us (63%)
  waiting for transfers between devices  334 us (20%)
  starting transfers between devices  143 us (8%)
  other arithmetic  60.3 us (4%)
  matrix products  49.9 us (3%)
  local copies, waits for them, and re-layouts  46.1 us (3%)
    all_gather x16, blocking collectives, gathered_products(): lax.all_gather(adjoint_rows.astype(jnp.bfloat16), 'feat', axis=0, tiled=T...  868 us
    all_to_all x15, waiting for transfers between devices, propagate(): lax.all_to_all(head_term.reshape(feat_count, rows_dev, model_width), 'fea...  281 us
    psum x1, blocking collectives, per_device(): lax.psum(enc_part.astype(jnp.bfloat16), 'feat').astype(jnp.float32)  205 us
    all_to_all x15, starting transfers between devices, propagate(): lax.all_to_all(head_term.reshape(feat_count, rows_dev, model_width), 'fea...  97.3 us
    ppermute x15, waiting for transfers between devices, shifted(): return lax.ppermute(shard, axis, pairs)  53.8 us
  transfers between devices with their start and end apart: 31, of which 30 were waited for; matrix products, arithmetic and copies ran while one was open for 3% of the time, Pallas kernels for 0%

commit v1 on v0

--- a/solution.py
+++ b/solution.py
@@ -1,9 +1,19 @@
+import functools
 import jax
 import jax.numpy as jnp
 from jax import lax
 from jax.sharding import PartitionSpec as P
 
 K_ACT = 256
+
+
+def turn_the_hubs(packet, shard_axis):
+    r1 = lax.all_gather(packet, axis_name=shard_axis)
+    prior = jnp.sum(r1, axis=0)
+    return prior
+
+
+play_flows = functools.partial(turn_the_hubs, shard_axis="feat")
 
 
 def shifted(shard, axis, by):
@@ -75,7 +85,7 @@
         jnp.bfloat16
     )
     enc_part = jnp.dot(target_pick, enc_table, preferred_element_type=jnp.float32)
-    enc_full = lax.psum(enc_part.astype(jnp.bfloat16), "feat").astype(jnp.float32)
+    enc_full = play_flows(enc_part.astype(jnp.bfloat16)).astype(jnp.float32)
     row_iota = feat_index * rows_dev + jnp.arange(rows_dev, dtype=jnp.int32)
     row_target = row_iota // seq_len
     row_pos = row_iota % seq_len

time: 1710 us -> 1630 us (0.953)
  blocking collectives: 1070 us -> 861 us
  waiting for transfers between devices: 334 us -> 451 us
    psum x1 -> x0, blocking collectives: 205 us -> none  [per_device(): lax.psum(enc_part.astype(jnp.bfloat16), 'feat').astype(jnp.float32)]
    all_gather x0 -> x1, waiting for transfers between devices: none -> 117 us  [turn_the_hubs(): r1 = lax.all_gather(packet, axis_name=shard_axis)]
  transfers between devices with their start and end apart: 31 -> 32, of which waited for: 30 -> 31; matrix products, arithmetic and copies ran while one was open for 3% -> 3% of each run, Pallas kernels for 0% -> 0%
where the time goes in v1:
time: 1630 us
  blocking collectives  861 us (53%)
  waiting for transfers between devices  451 us (28%)
  starting transfers between devices  141 us (9%)
  other arithmetic  62.5 us (4%)
  matrix products  50 us (3%)
  local copies, waits for them, and re-layouts  46.1 us (3%)
    all_gather x16, blocking collectives, gathered_products(): lax.all_gather(adjoint_rows.astype(jnp.bfloat16), 'feat', axis=0, tiled=T...  861 us
    all_to_all x15, waiting for transfers between devices, propagate(): lax.all_to_all(head_term.reshape(feat_count, rows_dev, model_width), 'fea...  280 us
    all_gather x1, waiting for transfers between devices, turn_the_hubs(): r1 = lax.all_gather(packet, axis_name=shard_axis)  117 us
    all_to_all x15, starting transfers between devices, propagate(): lax.all_to_all(head_term.reshape(feat_count, rows_dev, model_width), 'fea...  95.1 us
    ppermute x15, waiting for transfers between devices, shifted(): return lax.ppermute(shard, axis, pairs)  53.8 us
  transfers between devices with their start and end apart: 32, of which 31 were waited for; matrix products, arithmetic and copies ran while one was open for 3% of the time, Pallas kernels for 0%

profile of v1, /device:TPU:7, one launch (start us, length us, event | category | flops | bytes accessed | tf_op | source)
XLA Modules:
  0.0 1625.2 jit_solution(17540477301843990398)
XLA Ops:
  38.3 116.7 %all-gather.9.cloned.1.call-done = bf16[32,4,4608]{2,1,0:T(4,128)(2,1)} async-done(((bf16[1,4,4608]{2,1,0:T(4,128)(2,1)}), bf16[32,4,4608]{2,1,0:T(4,128)(2,1)}) %all-gather.9.cloned.1.call-update) | async-done | bytes 1179664 | tf_op jit(solution)/shard_map/all_gather | solution.py:11
  163.3 1397.4 %while.16 = (s32[]{:T(128)}, f32[2,4608]{1,0:T(2,128)S(1)}, f32[64,128]{1,0:T(8,128)}, bf16[128,4608]{1,0:T(8,128)(2,1)}, bf16[16,16]{0,1:T(8,128)(2,1)S(1)}, /*...) while((s32[]{:T(128)}, f32[2,4608]{1,0:T(2,128)S(1)}, ...), condition=%wide.region_9.10_spmd.clone, body=%wide.region_6.9_spmd.clone.sunk | while | flops 227964416 | bytes 15944625 | solution.py:154
  163.9 48.1 %all-gather.6 = bf16[32,2,4608]{2,1,0:T(2,128)(2,1)S(1)} all-gather(bf16[1,2,4608]{2,1,0:T(2,128)(2,1)S(1)} %convert_bitcast_fusion.3), channel_id=1, replica_groups=mesh['section'=16,'feat'=32] {'feat'}, dimensions={0}, use_global_device_ids=true | all-gather | bytes 608256 | tf_op jit(solution)/shard_map/while/body/eval_jaxpr/all_gather | solution.py:113
  254.0 54.0 %all-gather.6 = bf16[32,2,4608]{2,1,0:T(2,128)(2,1)S(1)} all-gather(bf16[1,2,4608]{2,1,0:T(2,128)(2,1)S(1)} %convert_bitcast_fusion.3), channel_id=1, replica_groups=mesh['section'=16,'feat'=32] {'feat'}, dimensions={0}, use_global_device_ids=true | all-gather | bytes 608256 | tf_op jit(solution)/shard_map/while/body/eval_jaxpr/all_gather | solution.py:113
  320.1 18.7 %all-to-all-done = bf16[32,2,4608]{2,1,0:T(2,128)(2,1)S(1)} async-done(((bf16[32,2,4608]{2,1,0:T(2,128)(2,1)}), bf16[32,2,4608]{2,1,0:T(2,128)(2,1)S(1)}, u32[]{:S(2)}, u32[]{:S(2)}) %all-to-all-start) | async-done | bytes 589856 | tf_op jit(solution)/shard_map/while/body/eval_jaxpr/all_to_all | solution.py:136
  347.5 54.1 %all-gather.6 = bf16[32,2,4608]{2,1,0:T(2,128)(2,1)S(1)} all-gather(bf16[1,2,4608]{2,1,0:T(2,128)(2,1)S(1)} %convert_bitcast_fusion.3), channel_id=1, replica_groups=mesh['section'=16,'feat'=32] {'feat'}, dimensions={0}, use_global_device_ids=true | all-gather | bytes 608256 | tf_op jit(solution)/shard_map/while/body/eval_jaxpr/all_gather | solution.py:113
  413.5 18.7 %all-to-all-done = bf16[32,2,4608]{2,1,0:T(2,128)(2,1)S(1)} async-done(((bf16[32,2,4608]{2,1,0:T(2,128)(2,1)}), bf16[32,2,4608]{2,1,0:T(2,128)(2,1)S(1)}, u32[]{:S(2)}, u32[]{:S(2)}) %all-to-all-start) | async-done | bytes 589856 | tf_op jit(solution)/shard_map/while/body/eval_jaxpr/all_to_all | solution.py:136
  440.8 54.1 %all-gather.6 = bf16[32,2,4608]{2,1,0:T(2,128)(2,1)S(1)} all-gather(bf16[1,2,4608]{2,1,0:T(2,128)(2,1)S(1)} %convert_bitcast_fusion.3), channel_id=1, replica_groups=mesh['section'=16,'feat'=32] {'feat'}, dimensions={0}, use_global_device_ids=true | all-gather | bytes 608256 | tf_op jit(solution)/shard_map/while/body/eval_jaxpr/all_gather | solution.py:113
  506.9 18.7 %all-to-all-done = bf16[32,2,4608]{2,1,0:T(2,128)(2,1)S(1)} async-done(((bf16[32,2,4608]{2,1,0:T(2,128)(2,1)}), bf16[32,2,4608]{2,1,0:T(2,128)(2,1)S(1)}, u32[]{:S(2)}, u32[]{:S(2)}) %all-to-all-start) | async-done | bytes 589856 | tf_op jit(solution)/shard_map/while/body/eval_jaxpr/all_to_all | solution.py:136
  534.2 54.2 %all-gather.6 = bf16[32,2,4608]{2,1,0:T(2,128)(2,1)S(1)} all-gather(bf16[1,2,4608]{2,1,0:T(2,128)(2,1)S(1)} %convert_bitcast_fusion.3), channel_id=1, replica_groups=mesh['section'=16,'feat'=32] {'feat'}, dimensions={0}, use_global_device_ids=true | all-gather | bytes 608256 | tf_op jit(solution)/shard_map/while/body/eval_jaxpr/all_gather | solution.py:113
  600.2 18.7 %all-to-all-done = bf16[32,2,4608]{2,1,0:T(2,128)(2,1)S(1)} async-done(((bf16[32,2,4608]{2,1,0:T(2,128)(2,1)}), bf16[32,2,4608]{2,1,0:T(2,128)(2,1)S(1)}, u32[]{:S(2)}, u32[]{:S(2)}) %all-to-all-start) | async-done | bytes 589856 | tf_op jit(solution)/shard_map/while/body/eval_jaxpr/all_to_all | solution.py:136
  627.6 54.2 %all-gather.6 = bf16[32,2,4608]{2,1,0:T(2,128)(2,1)S(1)} all-gather(bf16[1,2,4608]{2,1,0:T(2,128)(2,1)S(1)} %convert_bitcast_fusion.3), channel_id=1, replica_groups=mesh['section'=16,'feat'=32] {'feat'}, dimensions={0}, use_global_device_ids=true | all-gather | bytes 608256 | tf_op jit(solution)/shard_map/while/body/eval_jaxpr/all_gather | solution.py:113
  693.6 18.7 %all-to-all-done = bf16[32,2,4608]{2,1,0:T(2,128)(2,1)S(1)} async-done(((bf16[32,2,4608]{2,1,0:T(2,128)(2,1)}), bf16[32,2,4608]{2,1,0:T(2,128)(2,1)S(1)}, u32[]{:S(2)}, u32[]{:S(2)}) %all-to-all-start) | async-done | bytes 589856 | tf_op jit(solution)/shard_map/while/body/eval_jaxpr/all_to_all | solution.py:136
  721.0 54.2 %all-gather.6 = bf16[32,2,4608]{2,1,0:T(2,128)(2,1)S(1)} all-gather(bf16[1,2,4608]{2,1,0:T(2,128)(2,1)S(1)} %convert_bitcast_fusion.3), channel_id=1, replica_groups=mesh['section'=16,'feat'=32] {'feat'}, dimensions={0}, use_global_device_ids=true | all-gather | bytes 608256 | tf_op jit(solution)/shard_map/while/body/eval_jaxpr/all_gather | solution.py:113
  787.0 18.7 %all-to-all-done = bf16[32,2,4608]{2,1,0:T(2,128)(2,1)S(1)} async-done(((bf16[32,2,4608]{2,1,0:T(2,128)(2,1)}), bf16[32,2,4608]{2,1,0:T(2,128)(2,1)S(1)}, u32[]{:S(2)}, u32[]{:S(2)}) %all-to-all-start) | async-done | bytes 589856 | tf_op jit(solution)/shard_map/while/body/eval_jaxpr/all_to_all | solution.py:136
  814.3 54.2 %all-gather.6 = bf16[32,2,4608]{2,1,0:T(2,128)(2,1)S(1)} all-gather(bf16[1,2,4608]{2,1,0:T(2,128)(2,1)S(1)} %convert_bitcast_fusion.3), channel_id=1, replica_groups=mesh['section'=16,'feat'=32] {'feat'}, dimensions={0}, use_global_device_ids=true | all-gather | bytes 608256 | tf_op jit(solution)/shard_map/while/body/eval_jaxpr/all_gather | solution.py:113
  880.3 18.7 %all-to-all-done = bf16[32,2,4608]{2,1,0:T(2,128)(2,1)S(1)} async-done(((bf16[32,2,4608]{2,1,0:T(2,128)(2,1)}), bf16[32,2,4608]{2,1,0:T(2,128)(2,1)S(1)}, u32[]{:S(2)}, u32[]{:S(2)}) %all-to-all-start) | async-done | bytes 589856 | tf_op jit(solution)/shard_map/while/body/eval_jaxpr/all_to_all | solution.py:136
  907.7 54.2 %all-gather.6 = bf16[32,2,4608]{2,1,0:T(2,128)(2,1)S(1)} all-gather(bf16[1,2,4608]{2,1,0:T(2,128)(2,1)S(1)} %convert_bitcast_fusion.3), channel_id=1, replica_groups=mesh['section'=16,'feat'=32] {'feat'}, dimensions={0}, use_global_device_ids=true | all-gather | bytes 608256 | tf_op jit(solution)/shard_map/while/body/eval_jaxpr/all_gather | solution.py:113
  973.7 18.7 %all-to-all-done = bf16[32,2,4608]{2,1,0:T(2,128)(2,1)S(1)} async-done(((bf16[32,2,4608]{2,1,0:T(2,128)(2,1)}), bf16[32,2,4608]{2,1,0:T(2,128)(2,1)S(1)}, u32[]{:S(2)}, u32[]{:S(2)}) %all-to-all-start) | async-done | bytes 589856 | tf_op jit(solution)/shard_map/while/body/eval_jaxpr/all_to_all | solution.py:136
  1001.1 54.2 %all-gather.6 = bf16[32,2,4608]{2,1,0:T(2,128)(2,1)S(1)} all-gather(bf16[1,2,4608]{2,1,0:T(2,128)(2,1)S(1)} %convert_bitcast_fusion.3), channel_id=1, replica_groups=mesh['section'=16,'feat'=32] {'feat'}, dimensions={0}, use_global_device_ids=true | all-gather | bytes 608256 | tf_op jit(solution)/shard_map/while/body/eval_jaxpr/all_gather | solution.py:113
  1067.1 18.7 %all-to-all-done = bf16[32,2,4608]{2,1,0:T(2,128)(2,1)S(1)} async-done(((bf16[32,2,4608]{2,1,0:T(2,128)(2,1)}), bf16[32,2,4608]{2,1,0:T(2,128)(2,1)S(1)}, u32[]{:S(2)}, u32[]{:S(2)}) %all-to-all-start) | async-done | bytes 589856 | tf_op jit(solution)/shard_map/while/body/eval_jaxpr/all_to_all | solution.py:136
  1094.5 54.2 %all-gather.6 = bf16[32,2,4608]{2,1,0:T(2,128)(2,1)S(1)} all-gather(bf16[1,2,4608]{2,1,0:T(2,128)(2,1)S(1)} %convert_bitcast_fusion.3), channel_id=1, replica_groups=mesh['section'=16,'feat'=32] {'feat'}, dimensions={0}, use_global_device_ids=true | all-gather | bytes 608256 | tf_op jit(solution)/shard_map/while/body/eval_jaxpr/all_gather | solution.py:113
  1160.5 18.7 %all-to-all-done = bf16[32,2,4608]{2,1,0:T(2,128)(2,1)S(1)} async-done(((bf16[32,2,4608]{2,1,0:T(2,128)(2,1)}), bf16[32,2,4608]{2,1,0:T(2,128)(2,1)S(1)}, u32[]{:S(2)}, u32[]{:S(2)}) %all-to-all-start) | async-done | bytes 589856 | tf_op jit(solution)/shard_map/while/body/eval_jaxpr/all_to_all | solution.py:136
  1187.8 54.2 %all-gather.6 = bf16[32,2,4608]{2,1,0:T(2,128)(2,1)S(1)} all-gather(bf16[1,2,4608]{2,1,0:T(2,128)(2,1)S(1)} %convert_bitcast_fusion.3), channel_id=1, replica_groups=mesh['section'=16,'feat'=32] {'feat'}, dimensions={0}, use_global_device_ids=true | all-gather | bytes 608256 | tf_op jit(solution)/shard_map/while/body/eval_jaxpr/all_gather | solution.py:113
  1253.8 18.7 %all-to-all-done = bf16[32,2,4608]{2,1,0:T(2,128)(2,1)S(1)} async-done(((bf16[32,2,4608]{2,1,0:T(2,128)(2,1)}), bf16[32,2,4608]{2,1,0:T(2,128)(2,1)S(1)}, u32[]{:S(2)}, u32[]{:S(2)}) %all-to-all-start) | async-done | bytes 589856 | tf_op jit(solution)/shard_map/while/body/eval_jaxpr/all_to_all | solution.py:136
  1281.2 54.2 %all-gather.6 = bf16[32,2,4608]{2,1,0:T(2,128)(2,1)S(1)} all-gather(bf16[1,2,4608]{2,1,0:T(2,128)(2,1)S(1)} %convert_bitcast_fusion.3), channel_id=1, replica_groups=mesh['section'=16,'feat'=32] {'feat'}, dimensions={0}, use_global_device_ids=true | all-gather | bytes 608256 | tf_op jit(solution)/shard_map/while/body/eval_jaxpr/all_gather | solution.py:113
  1347.2 18.7 %all-to-all-done = bf16[32,2,4608]{2,1,0:T(2,128)(2,1)S(1)} async-done(((bf16[32,2,4608]{2,1,0:T(2,128)(2,1)}), bf16[32,2,4608]{2,1,0:T(2,128)(2,1)S(1)}, u32[]{:S(2)}, u32[]{:S(2)}) %all-to-all-start) | async-done | bytes 589856 | tf_op jit(solution)/shard_map/while/body/eval_jaxpr/all_to_all | solution.py:136
  1374.6 54.2 %all-gather.6 = bf16[32,2,4608]{2,1,0:T(2,128)(2,1)S(1)} all-gather(bf16[1,2,4608]{2,1,0:T(2,128)(2,1)S(1)} %convert_bitcast_fusion.3), channel_id=1, replica_groups=mesh['section'=16,'feat'=32] {'feat'}, dimensions={0}, use_global_device_ids=true | all-gather | bytes 608256 | tf_op jit(solution)/shard_map/while/body/eval_jaxpr/all_gather | solution.py:113
  1440.6 18.7 %all-to-all-done = bf16[32,2,4608]{2,1,0:T(2,128)(2,1)S(1)} async-done(((bf16[32,2,4608]{2,1,0:T(2,128)(2,1)}), bf16[32,2,4608]{2,1,0:T(2,128)(2,1)S(1)}, u32[]{:S(2)}, u32[]{:S(2)}) %all-to-all-start) | async-done | bytes 589856 | tf_op jit(solution)/shard_map/while/body/eval_jaxpr/all_to_all | solution.py:136
  1467.9 54.2 %all-gather.6 = bf16[32,2,4608]{2,1,0:T(2,128)(2,1)S(1)} all-gather(bf16[1,2,4608]{2,1,0:T(2,128)(2,1)S(1)} %convert_bitcast_fusion.3), channel_id=1, replica_groups=mesh['section'=16,'feat'=32] {'feat'}, dimensions={0}, use_global_device_ids=true | all-gather | bytes 608256 | tf_op jit(solution)/shard_map/while/body/eval_jaxpr/all_gather | solution.py:113
  1534.0 18.7 %all-to-all-done = bf16[32,2,4608]{2,1,0:T(2,128)(2,1)S(1)} async-done(((bf16[32,2,4608]{2,1,0:T(2,128)(2,1)}), bf16[32,2,4608]{2,1,0:T(2,128)(2,1)S(1)}, u32[]{:S(2)}, u32[]{:S(2)}) %all-to-all-start) | async-done | bytes 589856 | tf_op jit(solution)/shard_map/while/body/eval_jaxpr/all_to_all | solution.py:136
  1560.7 54.2 %all-gather.3 = bf16[32,2,4608]{2,1,0:T(2,128)(2,1)S(1)} all-gather(bf16[1,2,4608]{2,1,0:T(2,128)(2,1)S(1)} %convert_bitcast_fusion.1), channel_id=1, replica_groups=mesh['section'=16,'feat'=32] {'feat'}, dimensions={0}, use_global_device_ids=true | all-gather | bytes 608256 | tf_op jit(solution)/shard_map/all_gather | solution.py:113
  (351 shorter events, 371.9 us)
Async XLA Ops:
  14.1 144.9 %all-to-all-start.1 = ((bf16[32,8,4608]{2,1,0:T(8,128)(2,1)}), bf16[32,8,4608]{2,1,0:T(8,128)(2,1)S(1)}, u32[]{:S(2)}, u32[]{:S(2)}) async-start(bf16[32,8,4608]{2,1,0:T(8,128)(2,1)} %fusion.8), calls=%async_computation.1 | async-start | bytes 4718592 | tf_op jit(solution)/shard_map/all_to_all | solution.py:79
  30.6 124.4 %all-gather.9.cloned.1.call-start = ((), (), s32[]{:S(2)}) async-start(), calls=%async_computation.2 | async-start | bytes 1216512 | tf_op jit(solution)/shard_map/all_gather | solution.py:11
  216.6 28.8 %all-to-all-start = ((bf16[32,2,4608]{2,1,0:T(2,128)(2,1)}), bf16[32,2,4608]{2,1,0:T(2,128)(2,1)S(1)}, u32[]{:S(2)}, u32[]{:S(2)}) async-start(bf16[32,2,4608]{2,1,0:T(2,128)(2,1)} %reshape.321), calls=%async_computation | async-start | bytes 1179648 | tf_op jit(solution)/shard_map/while/body/eval_jaxpr/all_to_all | solution.py:136
  246.6 6.8 collective-permute-start
  312.6 26.1 %all-to-all-start = ((bf16[32,2,4608]{2,1,0:T(2,128)(2,1)}), bf16[32,2,4608]{2,1,0:T(2,128)(2,1)S(1)}, u32[]{:S(2)}, u32[]{:S(2)}) async-start(bf16[32,2,4608]{2,1,0:T(2,128)(2,1)} %reshape.321), calls=%async_computation | async-start | bytes 1179648 | tf_op jit(solution)/shard_map/while/body/eval_jaxpr/all_to_all | solution.py:136
  340.1 6.8 collective-permute-start
  406.1 26.1 %all-to-all-start = ((bf16[32,2,4608]{2,1,0:T(2,128)(2,1)}), bf16[32,2,4608]{2,1,0:T(2,128)(2,1)S(1)}, u32[]{:S(2)}, u32[]{:S(2)}) async-start(bf16[32,2,4608]{2,1,0:T(2,128)(2,1)} %reshape.321), calls=%async_computation | async-start | bytes 1179648 | tf_op jit(solution)/shard_map/while/body/eval_jaxpr/all_to_all | solution.py:136
  433.4 6.8 collective-permute-start
  499.5 26.1 %all-to-all-start = ((bf16[32,2,4608]{2,1,0:T(2,128)(2,1)}), bf16[32,2,4608]{2,1,0:T(2,128)(2,1)S(1)}, u32[]{:S(2)}, u32[]{:S(2)}) async-start(bf16[32,2,4608]{2,1,0:T(2,128)(2,1)} %reshape.321), calls=%async_computation | async-start | bytes 1179648 | tf_op jit(solution)/shard_map/while/body/eval_jaxpr/all_to_all | solution.py:136
  526.8 6.8 collective-permute-start
  593.0 25.9 %all-to-all-start = ((bf16[32,2,4608]{2,1,0:T(2,128)(2,1)}), bf16[32,2,4608]{2,1,0:T(2,128)(2,1)S(1)}, u32[]{:S(2)}, u32[]{:S(2)}) async-start(bf16[32,2,4608]{2,1,0:T(2,128)(2,1)} %reshape.321), calls=%async_computation | async-start | bytes 1179648 | tf_op jit(solution)/shard_map/while/body/eval_jaxpr/all_to_all | solution.py:136
  620.2 6.8 collective-permute-start
  686.3 25.9 %all-to-all-start = ((bf16[32,2,4608]{2,1,0:T(2,128)(2,1)}), bf16[32,2,4608]{2,1,0:T(2,128)(2,1)S(1)}, u32[]{:S(2)}, u32[]{:S(2)}) async-start(bf16[32,2,4608]{2,1,0:T(2,128)(2,1)} %reshape.321), calls=%async_computation | async-start | bytes 1179648 | tf_op jit(solution)/shard_map/while/body/eval_jaxpr/all_to_all | solution.py:136
  713.5 6.8 collective-permute-start
  779.7 26.0 %all-to-all-start = ((bf16[32,2,4608]{2,1,0:T(2,128)(2,1)}), bf16[32,2,4608]{2,1,0:T(2,128)(2,1)S(1)}, u32[]{:S(2)}, u32[]{:S(2)}) async-start(bf16[32,2,4608]{2,1,0:T(2,128)(2,1)} %reshape.321), calls=%async_computation | async-start | bytes 1179648 | tf_op jit(solution)/shard_map/while/body/eval_jaxpr/all_to_all | solution.py:136
  806.9 6.8 collective-permute-start
  873.1 25.9 %all-to-all-start = ((bf16[32,2,4608]{2,1,0:T(2,128)(2,1)}), bf16[32,2,4608]{2,1,0:T(2,128)(2,1)S(1)}, u32[]{:S(2)}, u32[]{:S(2)}) async-start(bf16[32,2,4608]{2,1,0:T(2,128)(2,1)} %reshape.321), calls=%async_computation | async-start | bytes 1179648 | tf_op jit(solution)/shard_map/while/body/eval_jaxpr/all_to_all | solution.py:136
  900.3 6.8 collective-permute-start
  966.4 26.0 %all-to-all-start = ((bf16[32,2,4608]{2,1,0:T(2,128)(2,1)}), bf16[32,2,4608]{2,1,0:T(2,128)(2,1)S(1)}, u32[]{:S(2)}, u32[]{:S(2)}) async-start(bf16[32,2,4608]{2,1,0:T(2,128)(2,1)} %reshape.321), calls=%async_computation | async-start | bytes 1179648 | tf_op jit(solution)/shard_map/while/body/eval_jaxpr/all_to_all | solution.py:136
  993.7 6.8 collective-permute-start
  1059.8 25.9 %all-to-all-start = ((bf16[32,2,4608]{2,1,0:T(2,128)(2,1)}), bf16[32,2,4608]{2,1,0:T(2,128)(2,1)S(1)}, u32[]{:S(2)}, u32[]{:S(2)}) async-start(bf16[32,2,4608]{2,1,0:T(2,128)(2,1)} %reshape.321), calls=%async_computation | async-start | bytes 1179648 | tf_op jit(solution)/shard_map/while/body/eval_jaxpr/all_to_all | solution.py:136
  1087.0 6.8 collective-permute-start
  1153.2 26.0 %all-to-all-start = ((bf16[32,2,4608]{2,1,0:T(2,128)(2,1)}), bf16[32,2,4608]{2,1,0:T(2,128)(2,1)S(1)}, u32[]{:S(2)}, u32[]{:S(2)}) async-start(bf16[32,2,4608]{2,1,0:T(2,128)(2,1)} %reshape.321), calls=%async_computation | async-start | bytes 1179648 | tf_op jit(solution)/shard_map/while/body/eval_jaxpr/all_to_all | solution.py:136
  1180.4 6.8 collective-permute-start
  1246.6 25.9 %all-to-all-start = ((bf16[32,2,4608]{2,1,0:T(2,128)(2,1)}), bf16[32,2,4608]{2,1,0:T(2,128)(2,1)S(1)}, u32[]{:S(2)}, u32[]{:S(2)}) async-start(bf16[32,2,4608]{2,1,0:T(2,128)(2,1)} %reshape.321), calls=%async_computation | async-start | bytes 1179648 | tf_op jit(solution)/shard_map/while/body/eval_jaxpr/all_to_all | solution.py:136
  1273.8 6.8 collective-permute-start
  1339.9 26.0 %all-to-all-start = ((bf16[32,2,4608]{2,1,0:T(2,128)(2,1)}), bf16[32,2,4608]{2,1,0:T(2,128)(2,1)S(1)}, u32[]{:S(2)}, u32[]{:S(2)}) async-start(bf16[32,2,4608]{2,1,0:T(2,128)(2,1)} %reshape.321), calls=%async_computation | async-start | bytes 1179648 | tf_op jit(solution)/shard_map/while/body/eval_jaxpr/all_to_all | solution.py:136
  1367.2 6.8 collective-permute-start
  1433.3 25.9 %all-to-all-start = ((bf16[32,2,4608]{2,1,0:T(2,128)(2,1)}), bf16[32,2,4608]{2,1,0:T(2,128)(2,1)S(1)}, u32[]{:S(2)}, u32[]{:S(2)}) async-start(bf16[32,2,4608]{2,1,0:T(2,128)(2,1)} %reshape.321), calls=%async_computation | async-start | bytes 1179648 | tf_op jit(solution)/shard_map/while/body/eval_jaxpr/all_to_all | solution.py:136
  1460.5 6.8 collective-permute-start
  1526.7 26.0 %all-to-all-start = ((bf16[32,2,4608]{2,1,0:T(2,128)(2,1)}), bf16[32,2,4608]{2,1,0:T(2,128)(2,1)S(1)}, u32[]{:S(2)}, u32[]{:S(2)}) async-start(bf16[32,2,4608]{2,1,0:T(2,128)(2,1)} %reshape.321), calls=%async_computation | async-start | bytes 1179648 | tf_op jit(solution)/shard_map/while/body/eval_jaxpr/all_to_all | solution.py:136
  1553.9 6.8 collective-permute-start
  (36 other events, 70.4 us)
Sparse Core Ops, SparseCore 0:
  34.7 120.2 all-gather.8
